TPU v7x, 32 devices: a whole 2x2x4 slice. The times are simulated.
32 devices in a mesh: occ: 4 (over x, core), vir: 8 (over z, y).
Axes of the slice: x: 2, y: 2, z: 4, core: 2. Of those that a mesh axis runs over, the one named last changes fastest.
Arguments:
- amplitudes: bfloat16 [8, 1024, 8, 1024], P(None, 'vir', 'occ'), may hold values from -0.0625 to 0.0625
- integrals: bfloat16 [8, 1024, 8, 1024], P(None, 'vir', 'occ'), may hold values from -6 to 6
- occ_irrep: int32 [8], replicated, may hold values from 0 to 1
- tile_irrep: int32 [8], replicated, may hold values from 0 to 1
Outputs:
- cycle_term: bfloat16 [8, 1024, 8, 1024], P('occ', 'vir')
Inputs may be any that keep to these rules, and one draw needn't show every extreme that they name: `occ_irrep`: irreps numbered as in D2h, so that the irrep of a product is the exclusive or of the numbers; the orbitals span the irreps 0 and 1. `tile_irrep`: irreps numbered as for occ_irrep.
All inputs are finite; a program needn't handle non-finite values.
Results may differ from a plain program's by a relative error of at most 0.001.
Values may be sent and summed in bfloat16 or wider, within the bound.
No kernel may reach another device: no remote copies, remote signals or barrier semaphores. Data moves between devices by JAX's collectives and lax.ppermute only.
A program may use at most 128 MiB of HBM per device.

v0:
```python
import jax
import jax.numpy as jnp
from jax import lax
from jax.sharding import PartitionSpec as P

TILE = 128


def lookup(values, positions):
    hits = positions[:, None] == jnp.arange(values.shape[0], dtype=jnp.int32)[None, :]
    return jnp.sum(jnp.where(hits, values[None, :], 0), axis=1)


def pair_codes(occ_irrep, tile_irrep, occ_rows, virt_rows):
    return jnp.bitwise_xor(
        lookup(occ_irrep, occ_rows)[:, None], lookup(tile_irrep, virt_rows // TILE)[None, :]
    )


def body(amplitudes, integrals, occ_irrep, tile_irrep):
    occ_total, vir_local, sum_local, virt_width = amplitudes.shape
    occ_index = lax.axis_index("occ")
    vir_index = lax.axis_index("vir")
    all_occ = jnp.arange(occ_total, dtype=jnp.int32)
    all_virt = jnp.arange(virt_width, dtype=jnp.int32)
    vir_rows = vir_index * vir_local + jnp.arange(vir_local, dtype=jnp.int32)
    sum_rows = occ_index * sum_local + jnp.arange(sum_local, dtype=jnp.int32)
    left_code = pair_codes(occ_irrep, tile_irrep, all_occ, vir_rows)
    right_code = pair_codes(occ_irrep, tile_irrep, sum_rows, all_virt)
    keep = left_code[:, :, None, None] == right_code[None, None, :, :]
    amplitudes = jnp.where(keep, amplitudes, jnp.zeros_like(amplitudes))
    integrals = jnp.where(keep, integrals, jnp.zeros_like(integrals))
    flat_amplitudes = amplitudes.reshape(occ_total * vir_local, sum_local * virt_width)
    shards = lax.all_gather(integrals, "vir", axis=1, tiled=True)
    block_count = shards.shape[1]
    shard_rows = shards.reshape(occ_total * block_count, sum_local * virt_width)
    product = lax.dot_general(
        flat_amplitudes, shard_rows, (((1,), (1,)), ((), ())), preferred_element_type=jnp.float32
    )
    partial_value = product.reshape(occ_total, vir_local, occ_total, block_count)
    summed = lax.psum_scatter(partial_value, "occ", scatter_dimension=0, tiled=True)
    mirrored = lax.all_to_all(
        lax.all_to_all(summed, "vir", split_axis=3, concat_axis=1, tiled=True),
        "occ",
        split_axis=2,
        concat_axis=0,
        tiled=True,
    )
    combined = summed + jnp.transpose(mirrored, (2, 3, 0, 1))
    return combined.astype(jnp.bfloat16)


def solution(mesh):
    placed = (P(None, "vir", "occ", None), P(None, "vir", "occ", None), P(), P())
    return jax.shard_map(
        body, mesh=mesh, in_specs=placed, out_specs=P("occ", "vir", None, None), check_vma=False
    )
```

profile of v0, /device:TPU:0, one launch (start us, length us, event | category | flops | bytes accessed | tf_op | source)
XLA Modules:
  0.0 1267.9 jit_solution(9547698494357062477)
XLA Ops:
  6.5 0.0 all-gather.2.cloned.1.call-start
  6.6 0.8 select_reduce_fusion.2
  7.3 0.8 fusion.14
  8.2 0.7 select_reduce_fusion.1
  8.9 0.7 select_reduce_fusion
  9.7 0.1 broadcast_xor_fusion.1
  9.7 0.1 broadcast_xor_fusion
  9.8 5.8 compare_select_fusion
  15.6 0.0 all-gather.2.cloned.1.call-update
  15.6 0.0 reduce-scatter.2.cloned.1.call-start
  15.6 640.5 %all-gather.2.cloned.1.call-done = bf16[8,1024,2,1024]{3,1,2,0:T(8,128)(2,1)} async-done(((bf16[8,128,2,1024]{3,1,2,0:T(8,128)(2,1)}), bf16[8,1024,2,1024]{3,1,2,0:T(8,128)(2,1)}) %all-gather.2.cloned.1.call-update) | async-done | bytes 33554448 | tf_op jit(solution)/shard_map/all_gather | solution.py:34
  656.2 42.0 %fusion.2 = f32[8,128,8,1024]{3,1,2,0:T(8,128)} fusion(bf16[8,1024,2,1024]{3,1,2,0:T(8,128)(2,1)} %all-gather.2.cloned.1.call-done, bf16[8,128,2,1024]{3,2,1,0:T(2,128)(2,1)} %param.4, s32[2,1024]{1,0:T(2,128)S(1)} %broadcast_xor_fusion, s32[8,128]{1,0:T(8,128)S(1)} %broadcast_xor_fusion.1), kind=kOutput, calls=%fused_computation.2 | convolution fusion | flops 34363932672 | bytes 71315456 | tf_op jit(solution)/shard_map/dot_general | solution.py:37
  698.2 0.0 reduce-scatter.2.cloned.1.call-update
  698.2 235.0 %reduce-scatter.2.cloned.1.call-done = f32[2,128,8,1024]{3,1,2,0:T(8,128)} async-done(((f32[8,128,8,1024]{3,1,2,0:T(8,128)}), f32[2,128,8,1024]{3,1,2,0:T(8,128)}) %reduce-scatter.2.cloned.1.call-update) | async-done | bytes 8388624 | tf_op jit(solution)/shard_map/reduce_scatter | solution.py:41
  933.2 9.2 copy.32
  942.4 189.0 %all_to_all.36 = f32[2,128,8,1024]{1,2,0,3:T(8,128)} all-to-all(f32[2,128,8,1024]{1,2,0,3:T(8,128)} %copy.32), channel_id=1, replica_groups=mesh['occ'=4,'vir'=8] {'vir'}, dimensions={3} | all-to-all | bytes 16777216 | tf_op jit(solution)/shard_map/all_to_all | solution.py:43
  1131.4 8.7 copy.42
  1140.1 100.6 %all_to_all.37 = f32[2,1024,8,128]{3,1,0,2:T(8,128)} all-to-all(f32[2,1024,8,128]{3,1,0,2:T(8,128)} %bitcast.26), channel_id=1, replica_groups=mesh['occ'=4,'vir'=8] {'occ'}, dimensions={2} | all-to-all | bytes 16777216 | tf_op jit(solution)/shard_map/all_to_all | solution.py:42
  1240.6 8.7 copy.37
  1249.4 7.3 add_convert_fusion
  1256.7 4.3 copy.38
  (3 shorter events, 0.0 us)
Async XLA Ops:
  6.5 649.7 %all-gather.2.cloned.1.call-start = ((), (), s32[]{:S(2)}) async-start(), calls=%async_computation.3 | async-start | bytes 37748736 | tf_op jit(solution)/shard_map/all_gather | solution.py:34
  15.6 917.6 %reduce-scatter.2.cloned.1.call-start = ((), (), s32[]{:S(2)}) async-start(), calls=%async_computation.4 | async-start | bytes 41943040 | tf_op jit(solution)/shard_map/reduce_scatter | solution.py:41
Sparse Core Ops, SparseCore 0:
  15.7 640.4 all-gather.1
  698.4 234.7 reduce-scatter.1
where the time goes:
time: 1270 us
  waiting for transfers between devices  876 us (69%)
  blocking collectives  290 us (23%)
  matrix products  42 us (3%)
  local copies, waits for them, and re-layouts  31 us (2%)
  other arithmetic  16.3 us (1%)
  between operations  13.4 us (1%)
    all_gather x1, waiting for transfers between devices, body(): shards = lax.all_gather(integrals, 'vir', axis=1, tiled=True)  641 us
    reduce_scatter x1, waiting for transfers between devices, body(): lax.psum_scatter(partial_value, 'occ', scatter_dimension=0, tiled=True)  235 us
    all_to_all x1, blocking collectives, body(): lax.all_to_all(summed, 'vir', split_axis=3, concat_axis=1, tiled=True)  189 us
    all_to_all x1, blocking collectives, body(): lax.all_to_all(lax.all_to_all(summed, 'vir', split_axis=3, concat_axis=1,...  101 us
    dot_general x1, matrix products, body(): lax.dot_general(flat_amplitudes, shard_rows, (((1,), (1,)), ((), ())), pr...  42 us
  transfers between devices with their start and end apart: 2, of which 2 were waited for; matrix products, arithmetic and copies ran while one was open for 0% of the time, Pallas kernels for 0%

commit v1 on v0

--- a/solution.py
+++ b/solution.py
@@ -1,9 +1,18 @@
+import functools
+
 import jax
 import jax.numpy as jnp
 from jax import lax
+from jax.experimental import pallas as pl
+from jax.experimental.pallas import tpu as pltpu
 from jax.sharding import PartitionSpec as P
 
 TILE = 128
+F32 = jnp.float32
+BF16 = jnp.bfloat16
+VMEM_LIMIT = 48 * 1024 * 1024
+SMEM_SPEC = pl.BlockSpec(memory_space=pltpu.SMEM)
+VMEM_SPEC = pl.BlockSpec(memory_space=pltpu.VMEM)
 
 
 def lookup(values, positions):
@@ -17,7 +26,7 @@
     )
 
 
-def body(amplitudes, integrals, occ_irrep, tile_irrep):
+def general_body(amplitudes, integrals, occ_irrep, tile_irrep):
     occ_total, vir_local, sum_local, virt_width = amplitudes.shape
     occ_index = lax.axis_index("occ")
     vir_index = lax.axis_index("vir")
@@ -50,8 +59,352 @@
     return combined.astype(jnp.bfloat16)
 
 
+def start(size, unit):
+    return pl.multiple_of(size * unit, unit)
+
+
+def pack_kernel(meta, occ, tile, w_ref, out_ref):
+    sum_local, rows, width = w_ref.shape
+    cts = width // TILE
+    own = tile[meta[1]]
+
+    def one(m, n):
+        j, k, c = m // (sum_local * cts), (m // cts) % sum_local, m % cts
+        ok = (occ[j] ^ own ^ occ[meta[0] * sum_local + k] ^ tile[c]) == 0
+
+        @pl.when(ok)
+        def _():
+            out_ref[n] = w_ref[k, pl.ds(start(j, TILE), TILE), pl.ds(start(c, TILE), TILE)]
+
+        return n + ok.astype(jnp.int32)
+
+    lax.fori_loop(0, (rows // TILE) * sum_local * cts, one, jnp.int32(0))
+
+
+def unpack(meta, occ, tile, their, pieces, wd):
+    sum_local, rows, width = wd.shape
+    cts = width // TILE
+    half = pieces[0].shape[0]
+
+    def one(m, n):
+        j, k, c = m // (sum_local * cts), (m // cts) % sum_local, m % cts
+        ok = (occ[j] ^ their ^ occ[meta[0] * sum_local + k] ^ tile[c]) == 0
+        where = (k, pl.ds(start(j, TILE), TILE), pl.ds(start(c, TILE), TILE))
+        if len(pieces) == 1:
+
+            @pl.when(ok)
+            def _():
+                wd[where] = pieces[0][n]
+        else:
+
+            @pl.when(ok & (n < half))
+            def _():
+                wd[where] = pieces[0][n]
+
+            @pl.when(ok & (n >= half))
+            def _():
+                wd[where] = pieces[1][n - half]
+
+        @pl.when(jnp.logical_not(ok))
+        def _():
+            wd[where] = jnp.zeros((TILE, TILE), wd.dtype)
+
+        return n + ok.astype(jnp.int32)
+
+    lax.fori_loop(0, (rows // TILE) * sum_local * cts, one, jnp.int32(0))
+
+
+def products(a_ref, b_ref, rows):
+    total = None
+    for k in range(a_ref.shape[0]):
+        part = lax.dot_general(
+            a_ref[k, rows, :], b_ref[k], (((1,), (1,)), ((), ())), preferred_element_type=F32
+        )
+        total = part if total is None else total + part
+    return total
+
+
+def block_kernel(modes, pieces, owners, slots, meta, occ, tile, t_ref, *refs):
+    count = len(modes) * pieces
+    w_refs, (keep_ref, send_ref, wd, blk) = refs[:count], refs[count:]
+    me = meta[0]
+    occ_total = t_ref.shape[1] // TILE
+    own_rows = occ_total // owners
+    span = own_rows * TILE
+    for place, mode in enumerate(modes):
+        their = tile[meta[3 + place]]
+        same = tile[meta[1]] ^ their
+        unpack(meta, occ, tile, their, w_refs[place * pieces : (place + 1) * pieces], wd)
+
+        def share(s, carry, mode=mode, same=same, place=place):
+            rows = pl.ds(start(s, span), span)
+            if mode == "lead":
+                blk[...] = products(t_ref, wd, rows)
+            elif mode == "follow":
+                blk[...] = products(wd, t_ref, rows)
+            elif mode == "self":
+                blk[...] = products(t_ref, wd, rows) + products(wd, t_ref, rows)
+            else:
+
+                @pl.when(meta[2] == 1)
+                def _():
+                    blk[...] = products(t_ref, wd, rows)
+
+                @pl.when(meta[2] != 1)
+                def _():
+                    blk[...] = products(wd, t_ref, rows)
+
+            other = s ^ me
+            far, near = other // 2, other % 2
+
+            def one(e, n):
+                ii, j = e // occ_total, e % occ_total
+                ok = (occ[s * own_rows + ii] ^ occ[j] ^ same) == 0
+                part = (pl.ds(start(ii, TILE), TILE), pl.ds(start(j, TILE), TILE))
+
+                @pl.when(ok & (near == 0))
+                def _():
+                    keep_ref[far, n] = blk[part]
+
+                @pl.when(ok & (near == 1))
+                def _():
+                    send_ref[far, n] = blk[part]
+
+                return n + ok.astype(jnp.int32)
+
+            lax.fori_loop(0, own_rows * occ_total, one, jnp.int32(place * slots))
+            return carry
+
+        lax.fori_loop(0, owners, share, 0)
+
+
+def mirror_kernel(meta, occ, tile, list_ref, *out_refs):
+    owners = len(out_refs)
+    own_rows = out_refs[0].shape[0]
+    occ_total = owners * own_rows
+    me = meta[0]
+    same = tile[meta[1]] ^ tile[meta[3]]
+
+    def one(e, n):
+        ii, j = e // occ_total, e % occ_total
+        ok = (occ[me * own_rows + ii] ^ occ[j] ^ same) == 0
+        rel = (j // own_rows) ^ me
+        block = list_ref[jnp.minimum(n, list_ref.shape[0] - 1)].astype(F32).T.astype(BF16)
+        block = jnp.where(ok, block, jnp.zeros_like(block))
+        for q in range(owners):
+
+            @pl.when(rel == q)
+            def _(q=q):
+                out_refs[q][j % own_rows, ii] = block
+
+        return n + ok.astype(jnp.int32)
+
+    lax.fori_loop(0, own_rows * occ_total, one, jnp.int32(0))
+
+
+def place_kernel(steps, half, owners, meta, occ, tile, *refs):
+    lists = refs[: steps + 1]
+    mirrored = refs[steps + 1 : -1]
+    out_ref = refs[-1]
+    own_rows, occ_total = out_ref.shape[:2]
+    me = meta[0]
+
+    def spread(list_ref, partner):
+        same = tile[meta[1]] ^ tile[partner]
+        cols = pl.ds(start(partner, TILE), TILE)
+
+        def one(e, n):
+            ii, j = e // occ_total, e % occ_total
+            ok = (occ[me * own_rows + ii] ^ occ[j] ^ same) == 0
+
+            @pl.when(ok)
+            def _():
+                out_ref[ii, j, :, cols] = list_ref[n].astype(BF16)
+
+            @pl.when(jnp.logical_not(ok))
+            def _():
+                out_ref[ii, j, :, cols] = jnp.zeros((TILE, TILE), BF16)
+
+            return n + ok.astype(jnp.int32)
+
+        lax.fori_loop(0, own_rows * occ_total, one, jnp.int32(0))
+
+    def lay(blocks, partner):
+        cols = pl.ds(start(partner, TILE), TILE)
+        for q in range(owners):
+            for jj in range(own_rows):
+                for ii in range(own_rows):
+                    out_ref[jj, (me ^ q) * own_rows + ii, :, cols] = blocks[q][jj, ii]
+
+    spread(lists[0], meta[1])
+    for t in range(1, steps + 1):
+        theirs = mirrored[(t - 1) * owners : t * owners]
+        if t == half:
+
+            @pl.when(meta[2] == 1)
+            def _(t=t):
+                spread(lists[t], meta[2 + t])
+
+            @pl.when(meta[2] != 1)
+            def _(t=t, theirs=theirs):
+                lay(theirs, meta[2 + steps + t])
+        else:
+            spread(lists[t], meta[2 + t])
+            lay(theirs, meta[2 + steps + t])
+
+
+def call(kernel, shapes, scalars, arrays, scratch=(), flops=0):
+    moved = sum(a.size * a.dtype.itemsize for a in arrays)
+    return pl.pallas_call(
+        kernel,
+        out_shape=shapes,
+        in_specs=[SMEM_SPEC] * len(scalars) + [VMEM_SPEC] * len(arrays),
+        out_specs=jax.tree.map(lambda _: VMEM_SPEC, shapes),
+        scratch_shapes=list(scratch),
+        compiler_params=pltpu.CompilerParams(vmem_limit_bytes=VMEM_LIMIT),
+        cost_estimate=pl.CostEstimate(flops=flops, bytes_accessed=2 * moved, transcendentals=0),
+    )(*scalars, *arrays)
+
+
+def ring_body(owners, size, cap, slots, t_rows, w_rows, occ_irrep, tile_irrep):
+    sum_local, rows, width = t_rows.shape
+    occ_total = rows // TILE
+    own_rows = occ_total // owners
+    half = size // 2
+    order = list(range(0, size, 2)) + list(range(size - 1, 0, -2))
+    ring = jnp.array(order, jnp.int32)
+    at = [order.index(v) for v in range(size)]
+    occ_index = lax.axis_index("occ").astype(jnp.int32)
+    vir_index = lax.axis_index("vir").astype(jnp.int32)
+    where = jnp.array(at, jnp.int32)[vir_index]
+    leads = (where < half).astype(jnp.int32)
+
+    def partner(shift):
+        return ring[(where + shift) % size]
+
+    def meta(*more):
+        return jnp.stack([occ_index, vir_index, leads, *more])
+
+    def hop(x, shift, only=None):
+        pairs = []
+        for o in range(owners):
+            for v in range(size):
+                if only is None or only(at[v]):
+                    pairs.append((o * size + v, o * size + order[(at[v] + shift) % size]))
+        return lax.ppermute(x, ("occ", "vir"), pairs)
+
+    def cross(x, rel):
+        pairs = [
+            (o * size + v, (o ^ rel) * size + v) for o in range(owners) for v in range(size)
+        ]
+        return lax.ppermute(x, ("occ", "vir"), pairs)
+
+    def shape(dims, dtype):
+        return jax.ShapeDtypeStruct(dims, dtype)
+
+    def blocks(modes, pieces, partners, ws):
+        n = len(modes) * slots
+        one = shape((owners // 2, n, TILE, TILE), F32)
+        product = 2 * rows * rows * width * sum_local
+        keep, send = call(
+            functools.partial(block_kernel, modes, pieces, owners, slots),
+            (one, one),
+            (meta(*partners), occ_irrep, tile_irrep),
+            (t_rows, *ws),
+            (pltpu.VMEM((sum_local, rows, width), BF16), pltpu.VMEM((own_rows * TILE, rows), F32)),
+            flops=product * sum(2 if m == "self" else 1 for m in modes),
+        )
+        got = cross(send, 1)
+        far = cross(keep[1] + got[1], 2)
+        return keep[0] + got[0] + far
+
+    def mirror(values, source):
+        out = shape((own_rows, own_rows, TILE, TILE), BF16)
+        parts = call(
+            mirror_kernel,
+            (out,) * owners,
+            (meta(source), occ_irrep, tile_irrep),
+            (values,),
+        )
+        return [parts[0]] + [cross(parts[q], q) for q in range(1, owners)]
+
+    packed = call(
+        pack_kernel,
+        shape((cap, TILE, TILE), BF16),
+        (meta(), occ_irrep, tile_irrep),
+        (w_rows,),
+    )
+    up, down = packed, packed
+    lists, mirrored = [], []
+    lists.append(blocks(("self",), 1, (vir_index,), (packed,)).astype(BF16))
+    for t in range(1, half):
+        up, down = hop(up, 1), hop(down, -1)
+        sums = blocks(("follow", "lead"), 1, (partner(-t), partner(t)), (up, down))
+        other = hop(sums[:slots], -t)
+        done = (sums[slots:] + other).astype(BF16)
+        lists.append(done)
+        mirrored += mirror(hop(done, t), partner(-t))
+    cut = cap // 2
+    first, second = hop(up[:cut], 1), hop(down[cut:], -1)
+    sums = blocks(("either",), 2, (partner(half),), (first, second))
+    other = hop(sums, half, lambda r: r >= half)
+    done = (sums + other).astype(BF16)
+    lists.append(done)
+    mirrored += mirror(hop(done, half, lambda r: r < half), partner(half))
+    partners = [partner(t) for t in range(1, half + 1)] + [partner(-t) for t in range(1, half + 1)]
+    out = call(
+        functools.partial(place_kernel, half, half, owners),
+        shape((own_rows, occ_total, TILE, size * TILE), BF16),
+        (meta(*partners), occ_irrep, tile_irrep),
+        (*lists, *mirrored),
+    )
+    return jnp.transpose(out, (0, 2, 1, 3))
+
+
+def body(owners, size, amplitudes, integrals, occ_irrep, tile_irrep):
+    occ_total, vir_local, sum_local, width = amplitudes.shape
+    rows = occ_total * vir_local
+    t_rows = jnp.transpose(amplitudes, (2, 0, 1, 3)).reshape(sum_local, rows, width)
+    w_rows = jnp.transpose(integrals, (2, 0, 1, 3)).reshape(sum_local, rows, width)
+    cts = width // TILE
+    ones, tiles = jnp.sum(occ_irrep), jnp.sum(tile_irrep)
+    zero = (occ_total - ones) * (cts - tiles) + ones * tiles
+    zero = jnp.maximum(zero, occ_total * cts - zero)
+    most = jnp.maximum(ones, occ_total - ones)
+    full = sum_local * occ_total * cts
+    own_rows = occ_total // owners
+    levels = [
+        (full // 2, own_rows * occ_total // 2),
+        (full // 2 + full // 16, own_rows * (occ_total // 2 + 1)),
+        (full // 2 + full // 8, own_rows * (occ_total // 2 + 2)),
+        (full, own_rows * occ_total),
+    ]
+    level = jnp.int32(len(levels) - 1)
+    for n in range(len(levels) - 2, -1, -1):
+        fits = (sum_local * zero <= levels[n][0]) & (own_rows * most <= levels[n][1])
+        level = jnp.where(fits, n, level)
+    return lax.switch(
+        level,
+        [functools.partial(ring_body, owners, size, cap, slots) for cap, slots in levels],
+        t_rows,
+        w_rows,
+        occ_irrep,
+        tile_irrep,
+    )
+
+
 def solution(mesh):
     placed = (P(None, "vir", "occ", None), P(None, "vir", "occ", None), P(), P())
-    return jax.shard_map(
-        body, mesh=mesh, in_specs=placed, out_specs=P("occ", "vir", None, None), check_vma=False
-    )
+    owners, size = mesh.shape["occ"], mesh.shape["vir"]
+
+    def whole(amplitudes, integrals, occ_irrep, tile_irrep):
+        one_tile = amplitudes.shape[1] == size * TILE and tile_irrep.shape[0] == size
+        if one_tile and owners == 4 and size % 2 == 0:
+            local = functools.partial(body, owners, size)
+        else:
+            local = general_body
+        return jax.shard_map(
+            local, mesh=mesh, in_specs=placed, out_specs=P("occ", "vir", None, None), check_vma=False
+        )(amplitudes, integrals, occ_irrep, tile_irrep)
+
+    return whole

time: 1270 us -> 490 us (0.39)
  waiting for transfers between devices: 876 us -> 184 us
  blocking collectives: 290 us -> 0 us
  Pallas kernels: 0 us -> 142 us
  starting transfers between devices: 0.04 us -> 77.9 us
  matrix products: 42 us -> 0 us
  loops' own time: 0 us -> 28.1 us
    all_gather x1 -> x0, waiting for transfers between devices: 641 us -> none  [body(): shards = lax.all_gather(integrals, 'vir', axis=1, tiled=True)]
    all_to_all x2 -> x0, blocking collectives: 290 us -> none  [the longest x1 189 us: body(): lax.all_to_all(summed, 'vir', split_axis=3, concat_axis=1, tiled=True)]
    reduce_scatter x1 -> x0, waiting for transfers between devices: 235 us -> none  [body(): lax.psum_scatter(partial_value, 'occ', scatter_dimension=0, tiled=True)]
    ppermute x0 -> x38, waiting for transfers between devices: none -> 184 us  [the longest x16 98.6 us: hop(): return lax.ppermute(x, ('occ', 'vir'), pairs)]
    pallas_call x0 -> x11, Pallas kernels: none -> 142 us  [call(): pl.pallas_call(kernel, out_shape=shapes, in_specs=[SMEM_SPEC] * len(scala...]
    ppermute x0 -> x38, starting transfers between devices: none -> 77.9 us  [the longest x16 62.9 us: hop(): return lax.ppermute(x, ('occ', 'vir'), pairs)]
    dot_general x1 -> x0, matrix products: 42 us -> none  [body(): lax.dot_general(flat_amplitudes, shard_rows, (((1,), (1,)), ((), ())), pr...]
    another operation x0 -> x1, loops' own time: none -> 28.1 us  [body(): lax.switch(level, [functools.partial(ring_body, owners, size, cap, slots)...]
  transfers between devices with their start and end apart: 2 -> 38, of which waited for: 2 -> 10; matrix products, arithmetic and copies ran while one was open for 0% -> 6% of each run, Pallas kernels for 0% -> 27%
where the time goes in v1:
time: 490 us; the launch traced here: 482 us
  waiting for transfers between devices  184 us (38%)
  Pallas kernels  142 us (29%)
  starting transfers between devices  77.9 us (16%)
  local copies, waits for them, and re-layouts  30.9 us (6%)
  loops' own time  28.1 us (6%)
  other arithmetic  15.5 us (3%)
    pallas_call x11, Pallas kernels, call(): pl.pallas_call(kernel, out_shape=shapes, in_specs=[SMEM_SPEC] * len(scala...  142 us
    ppermute x16, waiting for transfers between devices, hop(): return lax.ppermute(x, ('occ', 'vir'), pairs)  98.6 us
    ppermute x22, waiting for transfers between devices, cross(): return lax.ppermute(x, ('occ', 'vir'), pairs)  85.4 us
    ppermute x16, starting transfers between devices, hop(): return lax.ppermute(x, ('occ', 'vir'), pairs)  62.9 us
    another operation x1, loops' own time, body(): lax.switch(level, [functools.partial(ring_body, owners, size, cap, slots)...  28.1 us
    ppermute x22, starting transfers between devices, cross(): return lax.ppermute(x, ('occ', 'vir'), pairs)  15 us
  transfers between devices with their start and end apart: 38, of which 10 were waited for; matrix products, arithmetic and copies ran while one was open for 6% of the time, Pallas kernels for 27%

profile of v1, /device:TPU:0, one launch (start us, length us, event | category | flops | bytes accessed | tf_op | source)
XLA Modules:
  0.0 482.3 jit_solution(6708166301653604616)
XLA Ops:
  0.0 1.3 reduce_sum.18
  1.9 1.3 reduce_sum.19
  5.9 7.8 %copy_bitcast_fusion = (bf16[2,8,128,1024]{3,2,1,0:T(8,128)(2,1)}, bf16[2,8,128,1024]{3,2,1,0:T(8,128)(2,1)}) fusion(bf16[8,128,2,1024]{3,2,1,0:T(2,128)(2,1)} %param.16, bf16[8,128,2,1024]{3,2,1,0:T(2,128)(2,1)} %param.17), kind=kLoop, calls=%fused_computation.160 | loop fusion | bytes 16777216 | tf_op jit(solution)/shard_map/transpose | solution.py:367
  13.7 466.0 %conditional.1 = (bf16[2,128,8,1024]{3,2,1,0:T(8,128)(2,1)S(1)}) conditional(s32[]{:T(128)} %clamp.3, ((), (), s32[8]{0:T(128)S(1)}, s32[8]{0:T(128)S(1)}, bf16[2,8,128,1024]{3,2,1,0:T(8,128)(2,1)}, /*index=5*/bf16[2,8,128,1024]{3,2,1,0:T(8,128)(2,1)}) %tuple.89, ((), (), s32[8]{0:T(128)S(1)}, s32[8]{0:T(128)S(1)}, ...), branch_computations={%region_2.3_spmd, %region_3.4_spmd, %region_4.5_spmd, %region_5.6_... | conditional | flops 38663356416 | bytes 601361280 | solution.py:386
  13.7 1.3 dynamic_slice.56
  15.7 6.3 %branch_0_fun.11.refs_0_ = bf16[64,128,128]{2,1,0:T(8,128)(2,1)S(1)} custom-call(s32[3]{0:T(128)S(1)} %pad_add_fusion.2.meta, s32[8]{0:T(128)S(1)} %get-tuple-element.60.occ, s32[8]{0:T(128)S(1)} %get-tuple-element.61.tile, bf16[2,1024,1024]{2,1,0:T(8,128)(2,1)} %bitcast.184), custom_call_target="tpu_custom_call" | custom-call | bytes 8388608 | tf_op jit(solution)/shard_map/cond/branch_0_fun/pallas_call | solution.py:258
  22.0 3.1 collective-permute-start.2
  25.1 45.6 %collective-permute-done.2.refs_0_ = bf16[64,128,128]{2,1,0:T(8,128)(2,1)S(1)} collective-permute-done((bf16[64,128,128]{2,1,0:T(8,128)(2,1)S(1)}, bf16[64,128,128]{2,1,0:T(8,128)(2,1)S(1)}, u32[]{:S(2)}, u32[]{:S(2)}) %collective-permute-start.2) | collective-permute-done | bytes 2097184 | tf_op jit(solution)/shard_map/cond/branch_0_fun/ppermute | solution.py:294
  70.7 1.8 collective-permute-start.7
  72.5 1.3 collective-permute-start.8
  73.7 43.8 %collective-permute-done.7.refs_0_ = bf16[64,128,128]{2,1,0:T(8,128)(2,1)} collective-permute-done((bf16[64,128,128]{2,1,0:T(8,128)(2,1)S(1)}, bf16[64,128,128]{2,1,0:T(8,128)(2,1)}, u32[]{:S(2)}, u32[]{:S(2)}) %collective-permute-start.7) | collective-permute-done | bytes 2097184 | tf_op jit(solution)/shard_map/cond/branch_0_fun/ppermute | solution.py:294
  117.6 1.5 collective-permute-start.12
  119.1 1.3 collective-permute-start.13
  126.2 1.4 stack.98.meta
  127.6 1.3 stack.99.meta
  128.9 1.3 stack.100.meta
  131.0 1.9 pad_add_fusion.5
  132.9 27.0 %branch_0_fun.13 = (f32[2,16,128,128]{3,2,1,0:T(8,128)S(1)}, f32[2,16,128,128]{3,2,1,0:T(8,128)S(1)}) custom-call(s32[5]{0:T(128)S(1)} %stack.98.meta, s32[8]{0:T(128)S(1)} %get-tuple-element.60.occ, s32[8]{0:T(128)S(1)} %get-tuple-element.61.tile, bf16[2,1024,1024]{2,1,0:T(8,128)(2,1)} %bitcast.192, bf16[64,128,128]{2,1,0:T(8,128)(2,1)} %copy-done.69, ...), custom_call_target="tpu_custom_call" | custom-call | flops 8589934592 | bytes 16777216 | tf_op jit(solution)/shard_map/cond/branch_0_fun/pallas_call | solution.py:258
  160.0 28.4 %branch_0_fun.14 = (f32[2,16,128,128]{3,2,1,0:T(8,128)S(1)}, f32[2,16,128,128]{3,2,1,0:T(8,128)}) custom-call(s32[5]{0:T(128)S(1)} %stack.99.meta, s32[8]{0:T(128)S(1)} %get-tuple-element.60.occ, s32[8]{0:T(128)S(1)} %get-tuple-element.61.tile, bf16[2,1024,1024]{2,1,0:T(8,128)(2,1)} %bitcast.193, bf16[64,128,128]{2,1,0:T(8,128)(2,1)} %collective-permute-done.7.refs_0_, ...), custom_call_target="tpu_custom_call" | custom-call | flops 8589934592 | bytes 16777216 | tf_op jit(solution)/shard_map/cond/branch_0_fun/pallas_call | solution.py:258
  188.9 2.3 slice.350
  191.2 0.7 collective-permute-start.17
  191.9 2.4 slice.351
  194.3 1.5 collective-permute-start.18
  195.8 28.4 %branch_0_fun.15 = (f32[2,16,128,128]{3,2,1,0:T(8,128)S(1)}, f32[2,16,128,128]{3,2,1,0:T(8,128)}) custom-call(s32[5]{0:T(128)S(1)} %stack.100.meta, s32[8]{0:T(128)S(1)} %get-tuple-element.60.occ, s32[8]{0:T(128)S(1)} %get-tuple-element.61.tile, bf16[2,1024,1024]{2,1,0:T(8,128)(2,1)} %bitcast.194, bf16[64,128,128]{2,1,0:T(8,128)(2,1)} %collective-permute-done.12.refs_0_, ...), custom_call_target="tpu_custom_call" | custom-call | flops 8589934592 | bytes 16777216 | tf_op jit(solution)/shard_map/cond/branch_0_fun/pallas_call | solution.py:258
  224.2 19.3 %branch_0_fun.12 = (f32[2,8,128,128]{3,2,1,0:T(8,128)S(1)}, f32[2,8,128,128]{3,2,1,0:T(8,128)}) custom-call(s32[4]{0:T(128)S(1)} %get-tuple-element.223.meta, s32[8]{0:T(128)S(1)} %get-tuple-element.60.occ, s32[8]{0:T(128)S(1)} %get-tuple-element.61.tile, bf16[2,1024,1024]{2,1,0:T(8,128)(2,1)} %bitcast.195, bf16[64,128,128]{2,1,0:T(8,128)(2,1)S(1)} %branch_0_fun.11.refs_0_), custom_call_target="tpu_custom_call" | custom-call | flops 8589934592 | bytes 12582912 | tf_op jit(solution)/shard_map/cond/branch_0_fun/pallas_call | solution.py:258
  244.0 14.9 %branch_0_fun.16 = (f32[2,8,128,128]{3,2,1,0:T(8,128)S(1)}, f32[2,8,128,128]{3,2,1,0:T(8,128)S(1)}) custom-call(s32[4]{0:T(128)S(1)} %get-tuple-element.222.meta, s32[8]{0:T(128)S(1)} %get-tuple-element.60.occ, s32[8]{0:T(128)S(1)} %get-tuple-element.61.tile, bf16[2,1024,1024]{2,1,0:T(8,128)(2,1)} %bitcast.196, ...), custom_call_target="tpu_custom_call" | custom-call | flops 4294967296 | bytes 12582912 | tf_op jit(solution)/shard_map/cond/branch_0_fun/pallas_call | solution.py:258
  259.0 1.4 fusion.6
  260.3 1.6 collective-permute-start.5
  261.9 1.4 fusion.3
  263.9 1.6 collective-permute-start.1
  265.5 1.4 fusion
  267.5 1.6 collective-permute-start.20
  269.1 17.2 %collective-permute-done.5 = f32[16,128,128]{2,1,0:T(8,128)S(1)} collective-permute-done((f32[16,128,128]{2,1,0:T(8,128)S(1)}, f32[16,128,128]{2,1,0:T(8,128)S(1)}, u32[]{:S(2)}, u32[]{:S(2)}) %collective-permute-start.5) | collective-permute-done | bytes 1048608 | tf_op jit(solution)/shard_map/cond/branch_0_fun/ppermute | solution.py:300
  286.4 1.4 fusion.8
  287.8 1.6 collective-permute-start.6
  289.5 19.4 %collective-permute-done.10 = f32[16,128,128]{2,1,0:T(8,128)S(1)} collective-permute-done((f32[16,128,128]{2,1,0:T(8,128)S(1)}, f32[16,128,128]{2,1,0:T(8,128)S(1)}, u32[]{:S(2)}, u32[]{:S(2)}) %collective-permute-start.10) | collective-permute-done | bytes 1048608 | tf_op jit(solution)/shard_map/cond/branch_0_fun/ppermute | solution.py:300
  308.8 1.4 fusion.5
  310.3 2.6 collective-permute-start.11
  312.9 40.4 %collective-permute-done.20 = f32[8,128,128]{2,1,0:T(8,128)S(1)} collective-permute-done((f32[8,128,128]{2,1,0:T(8,128)S(1)}, f32[8,128,128]{2,1,0:T(8,128)S(1)}, u32[]{:S(2)}, u32[]{:S(2)}) %collective-permute-start.20) | collective-permute-done | bytes 524320 | tf_op jit(solution)/shard_map/cond/branch_0_fun/ppermute | solution.py:300
  353.5 1.3 collective-permute-start.21
  354.8 1.4 fusion.2
  356.3 3.8 collective-permute-start.16
  360.1 0.7 collective-permute-start.22
  360.9 2.9 collective-permute-start.26
  363.8 9.2 %collective-permute-done.21 = f32[8,128,128]{2,1,0:T(8,128)S(1)} collective-permute-done((f32[8,128,128]{2,1,0:T(8,128)S(1)}, f32[8,128,128]{2,1,0:T(8,128)S(1)}, u32[]{:S(2)}, u32[]{:S(2)}) %collective-permute-start.21) | collective-permute-done | bytes 524320 | tf_op jit(solution)/shard_map/cond/branch_0_fun/ppermute | solution.py:294
  373.1 1.4 collective-permute-start.34
  374.6 37.3 %collective-permute-start.30 = (bf16[8,128,128]{2,1,0:T(8,128)(2,1)S(1)}, bf16[8,128,128]{2,1,0:T(8,128)(2,1)S(1)}, u32[]{:S(2)}, u32[]{:S(2)}) collective-permute-start(bf16[8,128,128]{2,1,0:T(8,128)(2,1)S(1)} %fusion.12.refs_3_), channel_id=1, source_target_pairs={{0,6},{1,4},{2,7},{3,2},{4,5},{5,0},{6,3},{7,1},{8,14},{9,12},{10,... | collective-permute-start | bytes 786440 | tf_op jit(solution)/shard_map/cond/branch_0_fun/ppermute | solution.py:294
  411.9 3.1 branch_0_fun.17
  415.1 1.5 collective-permute-start.24
  416.6 3.3 branch_0_fun.18
  420.2 3.2 branch_0_fun.20
  424.3 1.5 collective-permute-start.28
  426.5 5.1 %stack.35.meta = s32[11]{0:T(128)S(1)} concatenate(s32[1]{0:T(128)} %bitcast, s32[1]{0:T(128)} %bitcast.1, s32[1]{0:T(128)S(6)} %convert_element_type.52, s32[1]{0:T(128)} %get-tuple-element.231, s32[1]{0:T(128)} %get-tuple-element.230, s32[1]{0:T(128)} %get-tuple-element.229, s32[1]{0:T(128)} %get-tuple-element.228, s32[1]{0:T(128)} %get-tuple-element.227, ...), dimensions={0} | concatenate | bytes 88 | tf_op jit(solution)/shard_map/cond/branch_0_fun/stack | solution.py:286
  431.5 2.5 branch_0_fun.19
  434.0 1.6 collective-permute-start.36
  436.3 1.5 collective-permute-start.32
  437.8 1.3 fusion.18.refs_0_
  439.1 1.6 collective-permute-done.36.refs_19_
  440.7 1.9 collective-permute-done.37.refs_20_
  442.6 3.7 collective-permute-done.32.refs_15_
  446.3 1.1 collective-permute-done.33.refs_16_
  447.4 5.8 %branch_0_fun.21 = bf16[2,8,128,1024]{3,2,1,0:T(8,128)(2,1)} custom-call(s32[11]{0:T(128)S(1)} %stack.35.meta, s32[8]{0:T(128)S(1)} %get-tuple-element.60.occ, s32[8]{0:T(128)S(1)} %get-tuple-element.61.tile, bf16[8,128,128]{2,1,0:T(8,128)(2,1)S(1)} %fusion.18.refs_0_, bf16[8,128,128]{2,1,0:T(8,128)(2,1)S(1)} %fusion.14.refs_1_, ...), custom_call_target="tpu_custom_call" | custom-call | bytes 6815744 | tf_op jit(solution)/shard_map/cond/branch_0_fun/pallas_call | solution.py:258
  453.2 4.5 copy.28
  479.8 2.0 copy-done.44
  (76 shorter events, 7.2 us)
Async XLA Ops:
  5.9 7.8 %copy-start.61 = (s32[8]{0:T(128)S(1)}, s32[8]{0:T(128)}, u32[]{:S(2)}) copy-start(s32[8]{0:T(128)} %param.18) | copy-start | bytes 100
  5.9 7.8 %copy-start.62 = (s32[8]{0:T(128)S(1)}, s32[8]{0:T(128)}, u32[]{:S(2)}) copy-start(s32[8]{0:T(128)} %param.19) | copy-start | bytes 100
  15.7 109.8 %copy-start.63 = (s32[8]{0:T(128)S(1)}, s32[8]{0:T(128)}, u32[]{:S(2)}) copy-start(s32[8]{0:T(128)} %constant.406.clone.1) | copy-start | bytes 100 | tf_op jit(solution)/shard_map/cond
  22.0 48.6 %collective-permute-start.2 = (bf16[64,128,128]{2,1,0:T(8,128)(2,1)S(1)}, bf16[64,128,128]{2,1,0:T(8,128)(2,1)S(1)}, u32[]{:S(2)}, u32[]{:S(2)}) collective-permute-start(bf16[64,128,128]{2,1,0:T(8,128)(2,1)S(1)} %branch_0_fun.11.refs_0_), channel_id=1, source_target_pairs={{0,2},{1,0},{2,4},{3,1},{4,6},{5,3},{6,7},{7,5},{8,10},{9,8},{10,1... | collective-permute-start | bytes 6291464 | tf_op jit(solution)/shard_map/cond/branch_0_fun/ppermute | solution.py:294
  25.1 47.4 %collective-permute-start.3 = (bf16[64,128,128]{2,1,0:T(8,128)(2,1)S(1)}, bf16[64,128,128]{2,1,0:T(8,128)(2,1)S(1)}, u32[]{:S(2)}, u32[]{:S(2)}) collective-permute-start(bf16[64,128,128]{2,1,0:T(8,128)(2,1)S(1)} %branch_0_fun.11.refs_0_), channel_id=1, source_target_pairs={{0,1},{1,3},{2,0},{3,5},{4,2},{5,7},{6,4},{7,6},{8,9},{9,11},{10,8... | collective-permute-start | bytes 6291464 | tf_op jit(solution)/shard_map/cond/branch_0_fun/ppermute | solution.py:294
  70.6 1.8 copy-start.69
  70.7 46.9 %collective-permute-start.7 = (bf16[64,128,128]{2,1,0:T(8,128)(2,1)S(1)}, bf16[64,128,128]{2,1,0:T(8,128)(2,1)}, u32[]{:S(2)}, u32[]{:S(2)}) collective-permute-start(bf16[64,128,128]{2,1,0:T(8,128)(2,1)S(1)} %collective-permute-done.2.refs_0_), channel_id=1, source_target_pairs={{0,2},{1,0},{2,4},{3,1},{4,6},{5,3},{6,7},{7,5},{8,10},{9,8},{10,1... | collective-permute-start | bytes 6291464 | tf_op jit(solution)/shard_map/cond/branch_0_fun/ppermute | solution.py:294
  72.5 45.1 %copy-start.70 = (bf16[64,128,128]{2,1,0:T(8,128)(2,1)}, bf16[64,128,128]{2,1,0:T(8,128)(2,1)S(1)}, u32[]{:S(2)}) copy-start(bf16[64,128,128]{2,1,0:T(8,128)(2,1)S(1)} %collective-permute-done.3.refs_1_) | copy-start | bytes 6291460 | tf_op jit(solution)/shard_map/cond
  72.5 46.6 %collective-permute-start.8 = (bf16[64,128,128]{2,1,0:T(8,128)(2,1)S(1)}, bf16[64,128,128]{2,1,0:T(8,128)(2,1)}, u32[]{:S(2)}, u32[]{:S(2)}) collective-permute-start(bf16[64,128,128]{2,1,0:T(8,128)(2,1)S(1)} %collective-permute-done.3.refs_1_), channel_id=1, source_target_pairs={{0,1},{1,3},{2,0},{3,5},{4,2},{5,7},{6,4},{7,6},{8,9},{9,11},{10,8... | collective-permute-start | bytes 6291464 | tf_op jit(solution)/shard_map/cond/branch_0_fun/ppermute | solution.py:294
  117.6 71.3 %collective-permute-start.12 = (bf16[64,128,128]{2,1,0:T(8,128)(2,1)}, bf16[64,128,128]{2,1,0:T(8,128)(2,1)}, u32[]{:S(2)}, u32[]{:S(2)}) collective-permute-start(bf16[64,128,128]{2,1,0:T(8,128)(2,1)} %collective-permute-done.7.refs_0_), channel_id=1, source_target_pairs={{0,2},{1,0},{2,4},{3,1},{4,6},{5,3},{6,7},{7,5},{8,10},{9,8},{10,1... | collective-permute-start | bytes 6291464 | tf_op jit(solution)/shard_map/cond/branch_0_fun/ppermute | solution.py:294
  119.1 72.9 %collective-permute-start.13 = (bf16[64,128,128]{2,1,0:T(8,128)(2,1)}, bf16[64,128,128]{2,1,0:T(8,128)(2,1)}, u32[]{:S(2)}, u32[]{:S(2)}) collective-permute-start(bf16[64,128,128]{2,1,0:T(8,128)(2,1)} %collective-permute-done.8.refs_1_), channel_id=1, source_target_pairs={{0,1},{1,3},{2,0},{3,5},{4,2},{5,7},{6,4},{7,6},{8,9},{9,11},{10,8... | collective-permute-start | bytes 6291464 | tf_op jit(solution)/shard_map/cond/branch_0_fun/ppermute | solution.py:294
  159.9 99.1 %collective-permute-start.4 = (f32[2,16,128,128]{3,2,1,0:T(8,128)S(1)}, f32[2,16,128,128]{3,2,1,0:T(8,128)}, u32[]{:S(2)}, u32[]{:S(2)}) collective-permute-start(f32[2,16,128,128]{3,2,1,0:T(8,128)S(1)} %get-tuple-element.67), channel_id=1, source_target_pairs={{0,8},{1,9},{2,10},{3,11},{4,12},{5,13},{6,14},{7,15},{8,0},{9,1},... | collective-permute-start | bytes 6291464 | tf_op jit(solution)/shard_map/cond/branch_0_fun/ppermute | solution.py:300
  188.4 73.5 %collective-permute-start.9 = (f32[2,16,128,128]{3,2,1,0:T(8,128)}, f32[2,16,128,128]{3,2,1,0:T(8,128)}, u32[]{:S(2)}, u32[]{:S(2)}) collective-permute-start(f32[2,16,128,128]{3,2,1,0:T(8,128)} %get-tuple-element.69), channel_id=1, source_target_pairs={{0,8},{1,9},{2,10},{3,11},{4,12},{5,13},{6,14},{7,15},{8,0},{9,1},... | collective-permute-start | bytes 6291464 | tf_op jit(solution)/shard_map/cond/branch_0_fun/ppermute | solution.py:300
  191.2 52.3 %collective-permute-start.17 = (bf16[32,128,128]{2,1,0:T(8,128)(2,1)}, bf16[32,128,128]{2,1,0:T(8,128)(2,1)S(1)}, u32[]{:S(2)}, u32[]{:S(2)}) collective-permute-start(bf16[32,128,128]{2,1,0:T(8,128)(2,1)} %slice.350), channel_id=1, source_target_pairs={{0,2},{1,0},{2,4},{3,1},{4,6},{5,3},{6,7},{7,5},{8,10},{9,8},{10,1... | collective-permute-start | bytes 3145736 | tf_op jit(solution)/shard_map/cond/branch_0_fun/ppermute | solution.py:294
  194.3 49.7 %collective-permute-start.18 = (bf16[32,128,128]{2,1,0:T(8,128)(2,1)}, bf16[32,128,128]{2,1,0:T(8,128)(2,1)S(1)}, u32[]{:S(2)}, u32[]{:S(2)}) collective-permute-start(bf16[32,128,128]{2,1,0:T(8,128)(2,1)} %slice.351), channel_id=1, source_target_pairs={{0,1},{1,3},{2,0},{3,5},{4,2},{5,7},{6,4},{7,6},{8,9},{9,11},{10,8... | collective-permute-start | bytes 3145736 | tf_op jit(solution)/shard_map/cond/branch_0_fun/ppermute | solution.py:294
  224.2 41.3 %collective-permute-start.14 = (f32[2,16,128,128]{3,2,1,0:T(8,128)}, f32[2,16,128,128]{3,2,1,0:T(8,128)}, u32[]{:S(2)}, u32[]{:S(2)}) collective-permute-start(f32[2,16,128,128]{3,2,1,0:T(8,128)} %get-tuple-element.71), channel_id=1, source_target_pairs={{0,8},{1,9},{2,10},{3,11},{4,12},{5,13},{6,14},{7,15},{8,0},{9,1},... | collective-permute-start | bytes 6291464 | tf_op jit(solution)/shard_map/cond/branch_0_fun/ppermute | solution.py:300
  243.5 20.4 %collective-permute-start = (f32[2,8,128,128]{3,2,1,0:T(8,128)}, f32[2,8,128,128]{3,2,1,0:T(8,128)S(1)}, u32[]{:S(2)}, u32[]{:S(2)}) collective-permute-start(f32[2,8,128,128]{3,2,1,0:T(8,128)} %get-tuple-element.65), channel_id=1, source_target_pairs={{0,8},{1,9},{2,10},{3,11},{4,12},{5,13},{6,14},{7,15},{8,0},{9,1},... | collective-permute-start | bytes 3145736 | tf_op jit(solution)/shard_map/cond/branch_0_fun/ppermute | solution.py:300
  258.9 8.6 %collective-permute-start.19 = (f32[2,8,128,128]{3,2,1,0:T(8,128)S(1)}, f32[2,8,128,128]{3,2,1,0:T(8,128)S(1)}, u32[]{:S(2)}, u32[]{:S(2)}) collective-permute-start(f32[2,8,128,128]{3,2,1,0:T(8,128)S(1)} %get-tuple-element.73), channel_id=1, source_target_pairs={{0,8},{1,9},{2,10},{3,11},{4,12},{5,13},{6,14},{7,15},{8,0},{9,1},... | collective-permute-start | bytes 3145736 | tf_op jit(solution)/shard_map/cond/branch_0_fun/ppermute | solution.py:300
  260.3 26.0 %collective-permute-start.5 = (f32[16,128,128]{2,1,0:T(8,128)S(1)}, f32[16,128,128]{2,1,0:T(8,128)S(1)}, u32[]{:S(2)}, u32[]{:S(2)}) collective-permute-start(f32[16,128,128]{2,1,0:T(8,128)S(1)} %fusion.6), channel_id=1, source_target_pairs={{0,16},{1,17},{2,18},{3,19},{4,20},{5,21},{6,22},{7,23},{8,24},{9,... | collective-permute-start | bytes 3145736 | tf_op jit(solution)/shard_map/cond/branch_0_fun/ppermute | solution.py:300
  263.3 45.6 %collective-permute-start.10 = (f32[16,128,128]{2,1,0:T(8,128)S(1)}, f32[16,128,128]{2,1,0:T(8,128)S(1)}, u32[]{:S(2)}, u32[]{:S(2)}) collective-permute-start(f32[16,128,128]{2,1,0:T(8,128)S(1)} %fusion.3), channel_id=1, source_target_pairs={{0,16},{1,17},{2,18},{3,19},{4,20},{5,21},{6,22},{7,23},{8,24},{9,... | collective-permute-start | bytes 3145736 | tf_op jit(solution)/shard_map/cond/branch_0_fun/ppermute | solution.py:300
  263.9 3.0 copy-start.57
  263.9 160.1 %collective-permute-start.1 = (f32[8,128,128]{2,1,0:T(8,128)S(1)}, f32[8,128,128]{2,1,0:T(8,128)S(1)}, u32[]{:S(2)}, u32[]{:S(2)}) collective-permute-start(f32[8,128,128]{2,1,0:T(8,128)S(1)} %fusion.15), channel_id=1, source_target_pairs={{0,16},{1,17},{2,18},{3,19},{4,20},{5,21},{6,22},{7,23},{8,24},{9,... | collective-permute-start | bytes 1572872 | tf_op jit(solution)/shard_map/cond/branch_0_fun/ppermute | solution.py:300
  266.9 87.9 %collective-permute-start.15 = (f32[16,128,128]{2,1,0:T(8,128)S(1)}, f32[16,128,128]{2,1,0:T(8,128)S(1)}, u32[]{:S(2)}, u32[]{:S(2)}) collective-permute-start(f32[16,128,128]{2,1,0:T(8,128)S(1)} %fusion), channel_id=1, source_target_pairs={{0,16},{1,17},{2,18},{3,19},{4,20},{5,21},{6,22},{7,23},{8,24},{9,... | collective-permute-start | bytes 3145736 | tf_op jit(solution)/shard_map/cond/branch_0_fun/ppermute | solution.py:300
  267.5 85.8 %collective-permute-start.20 = (f32[8,128,128]{2,1,0:T(8,128)S(1)}, f32[8,128,128]{2,1,0:T(8,128)S(1)}, u32[]{:S(2)}, u32[]{:S(2)}) collective-permute-start(f32[8,128,128]{2,1,0:T(8,128)S(1)} %fusion.9), channel_id=1, source_target_pairs={{0,16},{1,17},{2,18},{3,19},{4,20},{5,21},{6,22},{7,23},{8,24},{9,... | collective-permute-start | bytes 1572872 | tf_op jit(solution)/shard_map/cond/branch_0_fun/ppermute | solution.py:300
  287.8 72.2 %collective-permute-start.6 = (f32[8,128,128]{2,1,0:T(8,128)S(1)}, f32[8,128,128]{2,1,0:T(8,128)S(1)}, u32[]{:S(2)}, u32[]{:S(2)}) collective-permute-start(f32[8,128,128]{2,1,0:T(8,128)S(1)} %slice.341), channel_id=1, source_target_pairs={{0,1},{1,3},{2,0},{3,5},{4,2},{5,7},{6,4},{7,6},{8,9},{9,11},{10,8... | collective-permute-start | bytes 1572872 | tf_op jit(solution)/shard_map/cond/branch_0_fun/ppermute | solution.py:294
  310.3 50.6 %collective-permute-start.11 = (f32[8,128,128]{2,1,0:T(8,128)S(1)}, f32[8,128,128]{2,1,0:T(8,128)S(1)}, u32[]{:S(2)}, u32[]{:S(2)}) collective-permute-start(f32[8,128,128]{2,1,0:T(8,128)S(1)} %slice.345), channel_id=1, source_target_pairs={{0,3},{1,5},{2,1},{3,7},{4,0},{5,6},{6,2},{7,4},{8,11},{9,13},{10,... | collective-permute-start | bytes 1572872 | tf_op jit(solution)/shard_map/cond/branch_0_fun/ppermute | solution.py:294
  353.5 19.5 %collective-permute-start.21 = (f32[8,128,128]{2,1,0:T(8,128)S(1)}, f32[8,128,128]{2,1,0:T(8,128)S(1)}, u32[]{:S(2)}, u32[]{:S(2)}) collective-permute-start(f32[8,128,128]{2,1,0:T(8,128)S(1)} %fusion.11), channel_id=1, source_target_pairs={{1,6},{3,4},{5,2},{7,0},{9,14},{11,12},{13,10},{15,8},{17,22},{19,... | collective-permute-start | bytes 1572872 | tf_op jit(solution)/shard_map/cond/branch_0_fun/ppermute | solution.py:294
  356.3 18.2 %collective-permute-start.16 = (f32[8,128,128]{2,1,0:T(8,128)S(1)}, f32[8,128,128]{2,1,0:T(8,128)S(1)}, u32[]{:S(2)}, u32[]{:S(2)}) collective-permute-start(f32[8,128,128]{2,1,0:T(8,128)S(1)} %slice.349), channel_id=1, source_target_pairs={{0,5},{1,7},{2,3},{3,6},{4,1},{5,4},{6,0},{7,2},{8,13},{9,15},{10,... | collective-permute-start | bytes 1572872 | tf_op jit(solution)/shard_map/cond/branch_0_fun/ppermute | solution.py:294
  360.1 51.8 %collective-permute-start.22 = (bf16[8,128,128]{2,1,0:T(8,128)(2,1)S(1)}, bf16[8,128,128]{2,1,0:T(8,128)(2,1)S(1)}, u32[]{:S(2)}, u32[]{:S(2)}) collective-permute-start(bf16[8,128,128]{2,1,0:T(8,128)(2,1)S(1)} %fusion.14.refs_1_), channel_id=1, source_target_pairs={{0,2},{1,0},{2,4},{3,1},{4,6},{5,3},{6,7},{7,5},{8,10},{9,8},{10,1... | collective-permute-start | bytes 786440 | tf_op jit(solution)/shard_map/cond/branch_0_fun/ppermute | solution.py:294
  360.9 54.1 %collective-permute-start.26 = (bf16[8,128,128]{2,1,0:T(8,128)(2,1)S(1)}, bf16[8,128,128]{2,1,0:T(8,128)(2,1)S(1)}, u32[]{:S(2)}, u32[]{:S(2)}) collective-permute-start(bf16[8,128,128]{2,1,0:T(8,128)(2,1)S(1)} %fusion.13.refs_2_), channel_id=1, source_target_pairs={{0,4},{1,2},{2,6},{3,0},{4,7},{5,1},{6,5},{7,3},{8,12},{9,10},{10,... | collective-permute-start | bytes 786440 | tf_op jit(solution)/shard_map/cond/branch_0_fun/ppermute | solution.py:294
  373.1 46.8 %collective-permute-start.34 = (bf16[8,128,128]{2,1,0:T(8,128)(2,1)S(1)}, bf16[8,128,128]{2,1,0:T(8,128)(2,1)S(1)}, u32[]{:S(2)}, u32[]{:S(2)}) collective-permute-start(bf16[8,128,128]{2,1,0:T(8,128)(2,1)S(1)} %add_convert_fusion.refs_4_), channel_id=1, source_target_pairs={{0,7},{2,5},{4,3},{6,1},{8,15},{10,13},{12,11},{14,9},{16,23},{18,... | collective-permute-start | bytes 786440 | tf_op jit(solution)/shard_map/cond/branch_0_fun/ppermute | solution.py:294
  374.6 51.5 %collective-permute-start.30 = (bf16[8,128,128]{2,1,0:T(8,128)(2,1)S(1)}, bf16[8,128,128]{2,1,0:T(8,128)(2,1)S(1)}, u32[]{:S(2)}, u32[]{:S(2)}) collective-permute-start(bf16[8,128,128]{2,1,0:T(8,128)(2,1)S(1)} %fusion.12.refs_3_), channel_id=1, source_target_pairs={{0,6},{1,4},{2,7},{3,2},{4,5},{5,0},{6,3},{7,1},{8,14},{9,12},{10,... | collective-permute-start | bytes 786440 | tf_op jit(solution)/shard_map/cond/branch_0_fun/ppermute | solution.py:294
  415.0 9.2 %collective-permute-start.23 = (bf16[2,2,128,128]{3,2,1,0:T(8,128)(2,1)S(1)}, bf16[2,2,128,128]{3,2,1,0:T(8,128)(2,1)S(1)}, u32[]{:S(2)}, u32[]{:S(2)}) collective-permute-start(bf16[2,2,128,128]{3,2,1,0:T(8,128)(2,1)S(1)} %get-tuple-element.75), channel_id=1, source_target_pairs={{0,8},{1,9},{2,10},{3,11},{4,12},{5,13},{6,14},{7,15},{8,0},{9,1},... | collective-permute-start | bytes 393224 | tf_op jit(solution)/shard_map/cond/branch_0_fun/ppermute | solution.py:300
  415.1 10.7 %collective-permute-start.24 = (bf16[2,2,128,128]{3,2,1,0:T(8,128)(2,1)S(1)}, bf16[2,2,128,128]{3,2,1,0:T(8,128)(2,1)S(1)}, u32[]{:S(2)}, u32[]{:S(2)}) collective-permute-start(bf16[2,2,128,128]{3,2,1,0:T(8,128)(2,1)S(1)} %get-tuple-element.76), channel_id=1, source_target_pairs={{0,16},{1,17},{2,18},{3,19},{4,20},{5,21},{6,22},{7,23},{8,24},{9,... | collective-permute-start | bytes 393224 | tf_op jit(solution)/shard_map/cond/branch_0_fun/ppermute | solution.py:300
  419.8 14.2 %collective-permute-start.25 = (bf16[2,2,128,128]{3,2,1,0:T(8,128)(2,1)}, bf16[2,2,128,128]{3,2,1,0:T(8,128)(2,1)S(1)}, u32[]{:S(2)}, u32[]{:S(2)}) collective-permute-start(bf16[2,2,128,128]{3,2,1,0:T(8,128)(2,1)} %get-tuple-element.77), channel_id=1, source_target_pairs={{0,24},{1,25},{2,26},{3,27},{4,28},{5,29},{6,30},{7,31},{8,16},{9,... | collective-permute-start | bytes 393224 | tf_op jit(solution)/shard_map/cond/branch_0_fun/ppermute | solution.py:300
  423.3 0.7 copy-start.40
  424.0 1.8 copy-start.36
  424.0 2.4 copy-start.60
  424.0 11.6 %collective-permute-start.27 = (bf16[2,2,128,128]{3,2,1,0:T(8,128)(2,1)}, bf16[2,2,128,128]{3,2,1,0:T(8,128)(2,1)S(1)}, u32[]{:S(2)}, u32[]{:S(2)}) collective-permute-start(bf16[2,2,128,128]{3,2,1,0:T(8,128)(2,1)} %get-tuple-element.79), channel_id=1, source_target_pairs={{0,8},{1,9},{2,10},{3,11},{4,12},{5,13},{6,14},{7,15},{8,0},{9,1},... | collective-permute-start | bytes 393224 | tf_op jit(solution)/shard_map/cond/branch_0_fun/ppermute | solution.py:300
  424.3 11.3 %collective-permute-start.28 = (bf16[2,2,128,128]{3,2,1,0:T(8,128)(2,1)}, bf16[2,2,128,128]{3,2,1,0:T(8,128)(2,1)S(1)}, u32[]{:S(2)}, u32[]{:S(2)}) collective-permute-start(bf16[2,2,128,128]{3,2,1,0:T(8,128)(2,1)} %get-tuple-element.80), channel_id=1, source_target_pairs={{0,16},{1,17},{2,18},{3,19},{4,20},{5,21},{6,22},{7,23},{8,24},{9,... | collective-permute-start | bytes 393224 | tf_op jit(solution)/shard_map/cond/branch_0_fun/ppermute | solution.py:300
  425.8 10.5 %collective-permute-start.29 = (bf16[2,2,128,128]{3,2,1,0:T(8,128)(2,1)}, bf16[2,2,128,128]{3,2,1,0:T(8,128)(2,1)S(1)}, u32[]{:S(2)}, u32[]{:S(2)}) collective-permute-start(bf16[2,2,128,128]{3,2,1,0:T(8,128)(2,1)} %get-tuple-element.81), channel_id=1, source_target_pairs={{0,24},{1,25},{2,26},{3,27},{4,28},{5,29},{6,30},{7,31},{8,16},{9,... | collective-permute-start | bytes 393224 | tf_op jit(solution)/shard_map/cond/branch_0_fun/ppermute | solution.py:300
  426.0 11.7 %collective-permute-start.35 = (bf16[2,2,128,128]{3,2,1,0:T(8,128)(2,1)}, bf16[2,2,128,128]{3,2,1,0:T(8,128)(2,1)}, u32[]{:S(2)}, u32[]{:S(2)}) collective-permute-start(bf16[2,2,128,128]{3,2,1,0:T(8,128)(2,1)} %get-tuple-element.87), channel_id=1, source_target_pairs={{0,8},{1,9},{2,10},{3,11},{4,12},{5,13},{6,14},{7,15},{8,0},{9,1},... | collective-permute-start | bytes 393224 | tf_op jit(solution)/shard_map/cond/branch_0_fun/ppermute | solution.py:300
  434.0 6.6 %collective-permute-start.36 = (bf16[2,2,128,128]{3,2,1,0:T(8,128)(2,1)}, bf16[2,2,128,128]{3,2,1,0:T(8,128)(2,1)S(1)}, u32[]{:S(2)}, u32[]{:S(2)}) collective-permute-start(bf16[2,2,128,128]{3,2,1,0:T(8,128)(2,1)} %copy-done.40), channel_id=1, source_target_pairs={{0,16},{1,17},{2,18},{3,19},{4,20},{5,21},{6,22},{7,23},{8,24},{9,... | collective-permute-start | bytes 393224 | tf_op jit(solution)/shard_map/cond/branch_0_fun/ppermute | solution.py:300
  435.6 7.0 %collective-permute-start.37 = (bf16[2,2,128,128]{3,2,1,0:T(8,128)(2,1)}, bf16[2,2,128,128]{3,2,1,0:T(8,128)(2,1)S(1)}, u32[]{:S(2)}, u32[]{:S(2)}) collective-permute-start(bf16[2,2,128,128]{3,2,1,0:T(8,128)(2,1)} %copy-done.36), channel_id=1, source_target_pairs={{0,24},{1,25},{2,26},{3,27},{4,28},{5,29},{6,30},{7,31},{8,16},{9,... | collective-permute-start | bytes 393224 | tf_op jit(solution)/shard_map/cond/branch_0_fun/ppermute | solution.py:300
  435.6 7.0 %collective-permute-start.31 = (bf16[2,2,128,128]{3,2,1,0:T(8,128)(2,1)S(1)}, bf16[2,2,128,128]{3,2,1,0:T(8,128)(2,1)S(1)}, u32[]{:S(2)}, u32[]{:S(2)}) collective-permute-start(bf16[2,2,128,128]{3,2,1,0:T(8,128)(2,1)S(1)} %get-tuple-element.83), channel_id=1, source_target_pairs={{0,8},{1,9},{2,10},{3,11},{4,12},{5,13},{6,14},{7,15},{8,0},{9,1},... | collective-permute-start | bytes 393224 | tf_op jit(solution)/shard_map/cond/branch_0_fun/ppermute | solution.py:300
  436.3 10.0 %collective-permute-start.32 = (bf16[2,2,128,128]{3,2,1,0:T(8,128)(2,1)S(1)}, bf16[2,2,128,128]{3,2,1,0:T(8,128)(2,1)S(1)}, u32[]{:S(2)}, u32[]{:S(2)}) collective-permute-start(bf16[2,2,128,128]{3,2,1,0:T(8,128)(2,1)S(1)} %get-tuple-element.84), channel_id=1, source_target_pairs={{0,16},{1,17},{2,18},{3,19},{4,20},{5,21},{6,22},{7,23},{8,24},{9,... | collective-permute-start | bytes 393224 | tf_op jit(solution)/shard_map/cond/branch_0_fun/ppermute | solution.py:300
  437.8 9.6 %collective-permute-start.33 = (bf16[2,2,128,128]{3,2,1,0:T(8,128)(2,1)S(1)}, bf16[2,2,128,128]{3,2,1,0:T(8,128)(2,1)S(1)}, u32[]{:S(2)}, u32[]{:S(2)}) collective-permute-start(bf16[2,2,128,128]{3,2,1,0:T(8,128)(2,1)S(1)} %get-tuple-element.85), channel_id=1, source_target_pairs={{0,24},{1,25},{2,26},{3,27},{4,28},{5,29},{6,30},{7,31},{8,16},{9,... | collective-permute-start | bytes 393224 | tf_op jit(solution)/shard_map/cond/branch_0_fun/ppermute | solution.py:300
  479.8 2.0 copy-start.44
